TPU v7x, 32 devices: a whole 2x2x4 slice. The times are simulated.
32 devices in a mesh: rows: 8 (over z, y), layers: 4 (over x, core).
Axes of the slice: x: 2, y: 2, z: 4, core: 2. Of those that a mesh axis runs over, the one named last changes fastest.
Arguments:
- queries: bfloat16 [256, 4, 4096], P('rows', 'layers'), may hold values from -6 to 6
- precond: bfloat16 [4, 4096, 4096], P('layers', None, 'rows'), as said below
- train_grads: bfloat16 [16384, 4, 4096], P('rows', 'layers'), may hold values from -0.09375 to 0.09375
Outputs:
- scores: float32 [256, 16384], P('layers', 'rows')
Inputs may be any that keep to these rules, and one draw needn't show every extreme that they name: `precond`: symmetric in its last two dimensions.
All inputs are finite; a program needn't handle non-finite values.
Results may differ from a plain program's by a relative error of at most 0.0029.
Values may be sent and summed in bfloat16 or wider, within the bound.
A program may use at most 128 MiB of HBM per device.

v0:
```python
import jax
import jax.numpy as jnp
from jax import lax
from jax.sharding import PartitionSpec as P


def per_device(queries, precond, train_grads):
    all_queries = lax.all_gather(queries, "rows", axis=0, tiled=True)
    cond_cols = jnp.einsum(
        "qlf,lfc->qlc", all_queries, precond, preferred_element_type=jnp.float32
    ).astype(jnp.bfloat16)
    partial_scores = jnp.einsum(
        "qlc,tlc->qt",
        lax.all_gather(cond_cols, "rows", axis=2, tiled=True),
        train_grads,
        preferred_element_type=jnp.float32,
    )
    return lax.psum_scatter(partial_scores, "layers", scatter_dimension=0, tiled=True)


def solution(mesh):
    return jax.shard_map(
        per_device,
        mesh=mesh,
        in_specs=(P("rows", "layers", None), P("layers", None, "rows"), P("rows", "layers", None)),
        out_specs=P("layers", "rows"),
        check_vma=False,
    )
```

profile of v0, /device:TPU:0, one launch (start us, length us, event | category | flops | bytes accessed | tf_op | source)
XLA Modules:
  0.0 163.2 jit_solution(16461826900530594874)
XLA Ops:
  6.5 0.0 all-gather.3.cloned.1.call-start
  6.5 0.7 all-gather.3.cloned.1.call-update
  7.3 0.0 all-gather.5.cloned.1.call-start
  7.3 54.2 %all-gather.3.cloned.1.call-done = bf16[256,1,4096]{2,0,1:T(8,128)(2,1)} async-done(((bf16[32,1,4096]{2,0,1:T(8,128)(2,1)}), bf16[256,1,4096]{2,0,1:T(8,128)(2,1)}) %all-gather.3.cloned.1.call-update) | async-done | bytes 2097168 | tf_op jit(solution)/shard_map/all_gather | solution.py:8
  61.5 4.9 %fusion.11 = bf16[256,1,512]{0,2,1:T(8,128)(2,1)} fusion(bf16[256,1,4096]{2,0,1:T(8,128)(2,1)} %all-gather.3.cloned.1.call-done, bf16[1,4096,512]{2,1,0:T(8,128)(2,1)} %param.4), kind=kOutput, calls=%fused_computation.7 | convolution fusion | flops 1073872896 | bytes 6553600 | tf_op jit(solution)/shard_map/qlf,lfc->qlc/dot_general | solution.py:9
  66.4 0.0 all-gather.5.cloned.1.call-update
  66.4 0.0 reduce-scatter.2.cloned.1.call-start
  66.4 47.9 %all-gather.5.cloned.1.call-done = bf16[256,1,4096]{0,2,1:T(8,128)(2,1)} async-done(((bf16[256,1,512]{0,2,1:T(8,128)(2,1)}), bf16[256,1,4096]{0,2,1:T(8,128)(2,1)}) %all-gather.5.cloned.1.call-update) | async-done | bytes 2097168 | tf_op jit(solution)/shard_map/all_gather | solution.py:14
  114.3 12.3 %fusion = f32[256,2048]{1,0:T(8,128)} fusion(bf16[2048,1,4096]{2,0,1:T(8,128)(2,1)} %param.5, bf16[256,1,4096]{0,2,1:T(8,128)(2,1)} %all-gather.5.cloned.1.call-done), kind=kOutput, calls=%fused_computation | convolution fusion | flops 4294967296 | bytes 20971520 | tf_op jit(solution)/shard_map/qlc,tlc->qt/dot_general | solution.py:12
  126.6 0.0 reduce-scatter.2.cloned.1.call-update
  126.6 30.1 %reduce-scatter.2.cloned.1.call-done = f32[64,2048]{1,0:T(8,128)} async-done(((f32[256,2048]{1,0:T(8,128)}), f32[64,2048]{1,0:T(8,128)}) %reduce-scatter.2.cloned.1.call-update) | async-done | bytes 524304 | tf_op jit(solution)/shard_map/reduce_scatter | solution.py:18
Async XLA Ops:
  6.5 55.0 %all-gather.3.cloned.1.call-start = ((), (), s32[]{:S(2)}) async-start(), calls=%async_computation.1 | async-start | bytes 2359296 | tf_op jit(solution)/shard_map/all_gather | solution.py:8
  7.3 107.1 %all-gather.5.cloned.1.call-start = ((), (), s32[]{:S(2)}) async-start(), calls=%async_computation.2 | async-start | bytes 2359296 | tf_op jit(solution)/shard_map/all_gather | solution.py:14
  66.4 90.3 %reduce-scatter.2.cloned.1.call-start = ((), (), s32[]{:S(2)}) async-start(), calls=%async_computation.3 | async-start | bytes 2621440 | tf_op jit(solution)/shard_map/reduce_scatter | solution.py:18
Sparse Core Ops, SparseCore 0:
  9.5 51.9 all-gather.2
  66.5 47.7 all-gather.4
  126.8 29.8 reduce-scatter.1
where the time goes:
time: 163 us
  waiting for transfers between devices  133 us (82%)
  matrix products  17.1 us (10%)
  between operations  13.1 us (8%)
    all_gather x1, waiting for transfers between devices, per_device(): all_queries = lax.all_gather(queries, 'rows', axis=0, tiled=True)  54.2 us
    all_gather x1, waiting for transfers between devices, per_device(): lax.all_gather(cond_cols, 'rows', axis=2, tiled=True)  47.9 us
    reduce_scatter x1, waiting for transfers between devices, per_device(): lax.psum_scatter(partial_scores, 'layers', scatter_dimension=0, tiled=True)  30.1 us
    dot_general x1, matrix products, per_device(): jnp.einsum('qlc,tlc->qt', lax.all_gather(cond_cols, 'rows', axis=2, tiled...  12.3 us
    dot_general x1, matrix products, per_device(): jnp.einsum('qlf,lfc->qlc', all_queries, precond, preferred_element_type=j...  4.86 us
  transfers between devices with their start and end apart: 3, of which 3 were waited for; matrix products, arithmetic and copies ran while one was open for 0% of the time, Pallas kernels for 0%

commit v1 on v0

v1 whole, which is shorter than its diff:
```python
import functools

import jax
import jax.numpy as jnp
from jax import lax
from jax.experimental import pallas as pl
from jax.experimental.pallas import tpu as pltpu
from jax.sharding import PartitionSpec as P

MESH = pl.DeviceIdType.MESH
RIGHT, LEFT, ACROSS = 0, 1, 2


def kernel(
    line, q_hbm, p_hbm, t_hbm, out_ref,
    qbuf, cbuf, pv, tv, cacc, acc, crecv, xsend, xrecv,
    local_sem, send_sem, recv_sem, csend_sem, crecv_sem, xsend_sem, xrecv_sem,
):
    row, layer = lax.axis_index("rows"), lax.axis_index("layers")
    k, y = row // 2, row % 2
    x, core = layer // 2, layer % 2
    units, half_rows = qbuf.shape[1], qbuf.shape[2]
    width = cbuf.shape[3]
    nq = units * half_rows
    features, nt = tv.shape[1], tv.shape[0]
    has_right, has_left = k + 1 < line, k > 0

    def at_row(r):
        return {"rows": r, "layers": layer}

    def at_layer(l):
        return {"rows": row, "layers": l}

    right, left, across = at_row(row + 2), at_row(row - 2), at_row(2 * k + 1 - y)
    core_mate = at_layer(2 * x + 1 - core)
    x_mate = at_layer(2 * (1 - x) + core)

    load_q = [
        pltpu.make_async_copy(q_hbm.at[h], qbuf.at[h, row], local_sem.at[h])
        for h in range(2)
    ]
    load_p = pltpu.make_async_copy(p_hbm, pv, local_sem.at[2])
    load_t = pltpu.make_async_copy(t_hbm, tv, local_sem.at[3])
    load_q[0].start()
    load_q[1].start()
    load_p.start()

    barrier = pltpu.get_barrier_semaphore()
    for mate in (across, core_mate, x_mate):
        pl.semaphore_signal(barrier, inc=1, device_id=mate, device_id_type=MESH)

    @pl.when(has_right)
    def _():
        pl.semaphore_signal(barrier, inc=1, device_id=right, device_id_type=MESH)

    @pl.when(has_left)
    def _():
        pl.semaphore_signal(barrier, inc=1, device_id=left, device_id_type=MESH)

    neighbours = (k + line - 1) // line + (2 * line - 2 - k) // line
    pl.semaphore_wait(barrier, 3 + neighbours)

    def slot(phase, unit):
        return (qbuf if phase < 2 else cbuf).at[phase % 2, unit]

    def copy(phase, kk, side, target, own=False):
        unit = 2 * kk + y
        src = q_hbm.at[phase] if own and phase < 2 else slot(phase, unit)
        return pltpu.make_async_remote_copy(
            src_ref=src,
            dst_ref=slot(phase, unit),
            send_sem=send_sem.at[phase, side, kk],
            recv_sem=recv_sem.at[phase, unit],
            device_id=target,
            device_id_type=MESH,
        )

    def wait_unit(phase, unit):
        pltpu.make_async_remote_copy(
            src_ref=slot(phase, unit),
            dst_ref=slot(phase, unit),
            send_sem=send_sem.at[phase, ACROSS, 0],
            recv_sem=recv_sem.at[phase, unit],
            device_id=across,
            device_id_type=MESH,
        ).wait_recv()

    def open_phase(phase):
        @pl.when(has_right)
        def _():
            copy(phase, k, RIGHT, right, own=True).start()

        @pl.when(has_left)
        def _():
            copy(phase, k, LEFT, left, own=True).start()

        copy(phase, k, ACROSS, across, own=True).start()

    def forward(phase, s):
        @pl.when(k - s >= 0)
        def _():
            wait_unit(phase, 2 * (k - s) + y)

            @pl.when(has_right)
            def _():
                copy(phase, k - s, RIGHT, right).start()

            copy(phase, k - s, ACROSS, across).start()

        @pl.when(k + s < line)
        def _():
            wait_unit(phase, 2 * (k + s) + y)

            @pl.when(has_left)
            def _():
                copy(phase, k + s, LEFT, left).start()

            copy(phase, k + s, ACROSS, across).start()

    def forward_all(phase):
        lax.fori_loop(1, line, lambda s, c: (forward(phase, s), c)[1], 0)

    def wait_across(phase):
        lax.fori_loop(
            0, line, lambda kk, c: (wait_unit(phase, 2 * kk + 1 - y), c)[1], 0
        )

    depth = min(512, features)

    def condition(h):
        cacc[...] = jnp.zeros_like(cacc)

        def body(i, c):
            cut = pl.ds(pl.multiple_of(i * depth, depth), depth)
            cacc[...] += jnp.dot(
                qbuf[h, :, :, cut].reshape(nq, depth), pv[cut, :],
                preferred_element_type=jnp.float32,
            )
            return c

        lax.fori_loop(0, features // depth, body, 0)
        cbuf[h, row] = cacc[...].astype(jnp.bfloat16)

    tile = min(512, nt)

    def score(h, unit):
        cols = pl.ds(pl.multiple_of(unit * width, width), width)

        def body(i, c):
            rows = pl.ds(pl.multiple_of(i * tile, tile), tile)
            part = lax.dot_general(
                cbuf[h, unit], tv[rows, cols], (((1,), (1,)), ((), ())),
                preferred_element_type=jnp.float32,
            )
            acc[h, :, :, rows] += part.reshape(4, nq // 4, tile)
            return c

        lax.fori_loop(0, nt // tile, body, 0)

    def score_step(h, s):
        def both(kk):
            score(h, 2 * kk + y)
            wait_unit(2 + h, 2 * kk + 1 - y)
            score(h, 2 * kk + 1 - y)

        pl.when(k - s >= 0)(lambda: both(k - s))
        pl.when((s > 0) & (k + s < line))(lambda: both(k + s))

    def core_copy(h, xx):
        return pltpu.make_async_remote_copy(
            src_ref=acc.at[h, 2 * xx + 1 - core],
            dst_ref=crecv.at[h, xx],
            send_sem=csend_sem.at[h, xx],
            recv_sem=crecv_sem.at[h, xx],
            device_id=core_mate,
            device_id_type=MESH,
        )

    def x_copy(h):
        return pltpu.make_async_remote_copy(
            src_ref=xsend.at[h],
            dst_ref=xrecv.at[h],
            send_sem=xsend_sem.at[h],
            recv_sem=xrecv_sem.at[h],
            device_id=x_mate,
            device_id_type=MESH,
        )

    def reduce_open(h):
        core_copy(h, 1 - x).start()
        core_copy(h, x).start()

    def reduce_core(h):
        core_copy(h, 1 - x).wait_recv()
        xsend[h] = (acc[h, 2 * (1 - x) + core] + crecv[h, 1 - x]).astype(jnp.bfloat16)
        x_copy(h).start()

    def reduce_close(h):
        core_copy(h, x).wait_recv()
        x_copy(h).wait_recv()
        total = acc[h, layer] + crecv[h, x] + xrecv[h].astype(jnp.float32)
        out_ref[:, h] = total.reshape(out_ref.shape[0], half_rows, nt)

    open_phase(0)
    load_t.start()
    acc[...] = jnp.zeros_like(acc)
    forward_all(0)
    open_phase(1)
    load_q[0].wait()
    load_p.wait()
    wait_across(0)
    condition(0)
    forward_all(1)
    open_phase(2)
    load_q[1].wait()
    wait_across(1)
    condition(1)
    load_t.wait()

    def first(s, c):
        forward(2, s)
        score_step(0, s - 1)
        return c

    lax.fori_loop(1, line, first, 0)
    open_phase(3)
    score_step(0, line - 1)
    reduce_open(0)

    def second(s, c):
        forward(3, s)
        pl.when(s == 1)(lambda: reduce_core(0))
        score_step(1, s - 1)
        return c

    lax.fori_loop(1, line, second, 0)
    reduce_close(0)
    score_step(1, line - 1)
    reduce_open(1)
    reduce_core(1)
    reduce_close(1)

    for phase in range(4):

        def drain(kk, c):
            pl.when(has_right & (kk <= k))(
                lambda: copy(phase, kk, RIGHT, right).wait_send()
            )
            pl.when(has_left & (kk >= k))(
                lambda: copy(phase, kk, LEFT, left).wait_send()
            )
            copy(phase, kk, ACROSS, across).wait_send()
            return c

        lax.fori_loop(0, line, drain, 0)
    for h in range(2):
        core_copy(h, x).wait_send()
        core_copy(h, 1 - x).wait_send()
        x_copy(h).wait_send()


def per_device(units, queries, precond, train_grads):
    own, _, features = queries.shape
    width = precond.shape[2]
    nt = train_grads.shape[0]
    half_rows = own // 2
    nq = units * half_rows
    line = units // 2
    bf16, f32 = jnp.bfloat16, jnp.float32
    anywhere = pl.BlockSpec(memory_space=pl.ANY)
    flops = 2 * 2 * nq * features * (width + nt)
    out = pl.pallas_call(
        functools.partial(kernel, line),
        out_shape=jax.ShapeDtypeStruct((units // 4, 2, half_rows, nt), f32),
        in_specs=[anywhere] * 3,
        out_specs=pl.BlockSpec(memory_space=pltpu.VMEM),
        scratch_shapes=[
            pltpu.VMEM((2, units, half_rows, features), bf16),
            pltpu.VMEM((2, units, nq, width), bf16),
            pltpu.VMEM((features, width), bf16),
            pltpu.VMEM((nt, features), bf16),
            pltpu.VMEM((nq, width), f32),
            pltpu.VMEM((2, 4, nq // 4, nt), f32),
            pltpu.VMEM((2, 2, nq // 4, nt), f32),
            pltpu.VMEM((2, nq // 4, nt), bf16),
            pltpu.VMEM((2, nq // 4, nt), bf16),
            pltpu.SemaphoreType.DMA((4,)),
            pltpu.SemaphoreType.DMA((4, 3, line)),
            pltpu.SemaphoreType.DMA((4, units)),
            pltpu.SemaphoreType.DMA((2, 2)),
            pltpu.SemaphoreType.DMA((2, 2)),
            pltpu.SemaphoreType.DMA((2,)),
            pltpu.SemaphoreType.DMA((2,)),
        ],
        compiler_params=pltpu.CompilerParams(
            collective_id=0, has_side_effects=True, vmem_limit_bytes=60 << 20
        ),
        cost_estimate=pl.CostEstimate(
            flops=flops, bytes_accessed=2 * features * (width + nt), transcendentals=0
        ),
    )(
        queries.reshape(2, half_rows, features),
        precond.reshape(features, width),
        train_grads.reshape(nt, features),
    )
    return out.reshape(2 * units // 4 * half_rows, nt)


def solution(mesh):
    return jax.shard_map(
        functools.partial(per_device, mesh.shape["rows"]),
        mesh=mesh,
        in_specs=(P("rows", "layers", None), P("layers", None, "rows"), P("rows", "layers", None)),
        out_specs=P("layers", "rows"),
        check_vma=False,
    )
```

time: 163 us -> 73.2 us (0.45)
  waiting for transfers between devices: 133 us -> 0 us
  Pallas kernels: 0 us -> 70.9 us
  matrix products: 17.1 us -> 0 us
  between operations: 13.1 us -> 0.01 us
  local copies, waits for them, and re-layouts: 0 us -> 1.87 us
    all_gather x2 -> x0, waiting for transfers between devices: 102 us -> none  [the longest x1 54.2 us: per_device(): all_queries = lax.all_gather(queries, 'rows', axis=0, tiled=True)]
    pallas_call x0 -> x1, Pallas kernels: none -> 70.9 us  [per_device(): pl.pallas_call(functools.partial(kernel, line), out_shape=jax.ShapeDtypeS...]
    reduce_scatter x1 -> x0, waiting for transfers between devices: 30.1 us -> none  [per_device(): lax.psum_scatter(partial_scores, 'layers', scatter_dimension=0, tiled=True)]
    dot_general x2 -> x0, matrix products: 17.1 us -> none  [the longest x1 12.3 us: per_device(): jnp.einsum('qlc,tlc->qt', lax.all_gather(cond_cols, 'rows', axis=2, tiled...]
    unnamed x0 -> x1, local copies, waits for them, and re-layouts: none -> 1.87 us
  transfers between devices with their start and end apart: 3 -> 0, of which waited for: 3 -> 0; matrix products, arithmetic and copies ran while one was open for 0% -> 0% of each run, Pallas kernels for 0% -> 0%
where the time goes in v1:
time: 73.2 us; the launch traced here: 72.8 us
  Pallas kernels  70.9 us (97%)
  local copies, waits for them, and re-layouts  1.87 us (3%)
    pallas_call x1, Pallas kernels, per_device(): pl.pallas_call(functools.partial(kernel, line), out_shape=jax.ShapeDtypeS...  70.9 us
    unnamed x1, local copies, waits for them, and re-layouts  1.87 us

profile of v1, /device:TPU:0, one launch (start us, length us, event | category | flops | bytes accessed | tf_op | source)
XLA Modules:
  0.0 72.8 jit_solution(456429742967714171)
XLA Ops:
  0.0 70.9 %shard_map.37 = f32[2,2,16,2048]{3,2,1,0:T(8,128)} custom-call(bf16[2,16,4096]{2,1,0:T(8,128)(2,1)} %bitcast.7, bf16[4096,512]{1,0:T(8,128)(2,1)} %bitcast.5, bf16[2048,4096]{1,0:T(8,128)(2,1)} %bitcast.4), custom_call_target="tpu_custom_call" | custom-call | flops 5368709120 | bytes 20971520 | tf_op jit(solution)/shard_map/pallas_call | solution.py:272
  70.9 1.9 %copy.5 = f32[64,2048]{1,0:T(8,128)} copy(f32[64,2048]{1,0:T(8,128)} %bitcast.6) | data formatting | bytes 1048576

commit v2 on v1

--- a/solution.py
+++ b/solution.py
@@ -8,7 +8,7 @@
 from jax.sharding import PartitionSpec as P
 
 MESH = pl.DeviceIdType.MESH
-RIGHT, LEFT, ACROSS = 0, 1, 2
+ALONG, ACROSS = 0, 1
 
 
 def kernel(
@@ -23,7 +23,6 @@
     width = cbuf.shape[3]
     nq = units * half_rows
     features, nt = tv.shape[1], tv.shape[0]
-    has_right, has_left = k + 1 < line, k > 0
 
     def at_row(r):
         return {"rows": r, "layers": layer}
@@ -31,7 +30,7 @@
     def at_layer(l):
         return {"rows": row, "layers": l}
 
-    right, left, across = at_row(row + 2), at_row(row - 2), at_row(2 * k + 1 - y)
+    across = at_row(2 * k + 1 - y)
     core_mate = at_layer(2 * x + 1 - core)
     x_mate = at_layer(2 * (1 - x) + core)
 
@@ -49,29 +48,42 @@
     for mate in (across, core_mate, x_mate):
         pl.semaphore_signal(barrier, inc=1, device_id=mate, device_id_type=MESH)
 
-    @pl.when(has_right)
-    def _():
-        pl.semaphore_signal(barrier, inc=1, device_id=right, device_id_type=MESH)
-
-    @pl.when(has_left)
-    def _():
-        pl.semaphore_signal(barrier, inc=1, device_id=left, device_id_type=MESH)
-
-    neighbours = (k + line - 1) // line + (2 * line - 2 - k) // line
-    pl.semaphore_wait(barrier, 3 + neighbours)
+    def each_on_line(act):
+        def body(kk, c):
+            pl.when(kk != k)(lambda: act(kk))
+            return c
+
+        lax.fori_loop(0, line, body, 0)
+
+    def greet(kk):
+        pl.semaphore_signal(
+            barrier, inc=1, device_id=at_row(2 * kk + y), device_id_type=MESH
+        )
+
+    each_on_line(greet)
+    pl.semaphore_wait(barrier, 3 + line - 1)
 
     def slot(phase, unit):
         return (qbuf if phase < 2 else cbuf).at[phase % 2, unit]
 
-    def copy(phase, kk, side, target, own=False):
+    def along(phase, kk):
+        return pltpu.make_async_remote_copy(
+            src_ref=q_hbm.at[phase] if phase < 2 else slot(phase, row),
+            dst_ref=slot(phase, row),
+            send_sem=send_sem.at[phase, ALONG, kk],
+            recv_sem=recv_sem.at[phase, row],
+            device_id=at_row(2 * kk + y),
+            device_id_type=MESH,
+        )
+
+    def relay_copy(phase, kk, own=False):
         unit = 2 * kk + y
-        src = q_hbm.at[phase] if own and phase < 2 else slot(phase, unit)
         return pltpu.make_async_remote_copy(
-            src_ref=src,
+            src_ref=q_hbm.at[phase] if own and phase < 2 else slot(phase, unit),
             dst_ref=slot(phase, unit),
-            send_sem=send_sem.at[phase, side, kk],
+            send_sem=send_sem.at[phase, ACROSS, kk],
             recv_sem=recv_sem.at[phase, unit],
-            device_id=target,
+            device_id=across,
             device_id_type=MESH,
         )
 
@@ -86,39 +98,25 @@
         ).wait_recv()
 
     def open_phase(phase):
-        @pl.when(has_right)
-        def _():
-            copy(phase, k, RIGHT, right, own=True).start()
-
-        @pl.when(has_left)
-        def _():
-            copy(phase, k, LEFT, left, own=True).start()
-
-        copy(phase, k, ACROSS, across, own=True).start()
-
-    def forward(phase, s):
-        @pl.when(k - s >= 0)
-        def _():
-            wait_unit(phase, 2 * (k - s) + y)
-
-            @pl.when(has_right)
-            def _():
-                copy(phase, k - s, RIGHT, right).start()
-
-            copy(phase, k - s, ACROSS, across).start()
-
-        @pl.when(k + s < line)
-        def _():
-            wait_unit(phase, 2 * (k + s) + y)
-
-            @pl.when(has_left)
-            def _():
-                copy(phase, k + s, LEFT, left).start()
-
-            copy(phase, k + s, ACROSS, across).start()
-
-    def forward_all(phase):
-        lax.fori_loop(1, line, lambda s, c: (forward(phase, s), c)[1], 0)
+        relay_copy(phase, k, own=True).start()
+
+        def body(d, c):
+            pl.when(k + d < line)(lambda: along(phase, k + d).start())
+            pl.when(k - d >= 0)(lambda: along(phase, k - d).start())
+            return c
+
+        lax.fori_loop(1, line, body, 0)
+
+    def relay(phase, s):
+        def one(kk):
+            wait_unit(phase, 2 * kk + y)
+            relay_copy(phase, kk).start()
+
+        pl.when(k - s >= 0)(lambda: one(k - s))
+        pl.when(k + s < line)(lambda: one(k + s))
+
+    def relay_rest(phase, start):
+        lax.fori_loop(start, line, lambda s, c: (relay(phase, s), c)[1], 0)
 
     def wait_across(phase):
         lax.fori_loop(
@@ -157,14 +155,17 @@
 
         lax.fori_loop(0, nt // tile, body, 0)
 
-    def score_step(h, s):
-        def both(kk):
-            score(h, 2 * kk + y)
+    def score_line(h, s):
+        pl.when(k - s >= 0)(lambda: score(h, 2 * (k - s) + y))
+        pl.when((s > 0) & (k + s < line))(lambda: score(h, 2 * (k + s) + y))
+
+    def score_across(h, s):
+        def one(kk):
             wait_unit(2 + h, 2 * kk + 1 - y)
             score(h, 2 * kk + 1 - y)
 
-        pl.when(k - s >= 0)(lambda: both(k - s))
-        pl.when((s > 0) & (k + s < line))(lambda: both(k + s))
+        pl.when(k - s >= 0)(lambda: one(k - s))
+        pl.when((s > 0) & (k + s < line))(lambda: one(k + s))
 
     def core_copy(h, xx):
         return pltpu.make_async_remote_copy(
@@ -204,52 +205,51 @@
     open_phase(0)
     load_t.start()
     acc[...] = jnp.zeros_like(acc)
-    forward_all(0)
+    relay(0, 1)
     open_phase(1)
+    relay_rest(0, 2)
     load_q[0].wait()
     load_p.wait()
     wait_across(0)
+    relay(1, 1)
     condition(0)
-    forward_all(1)
     open_phase(2)
+    relay_rest(1, 2)
     load_q[1].wait()
     wait_across(1)
+    relay(2, 1)
     condition(1)
+    open_phase(3)
+    relay_rest(2, 2)
     load_t.wait()
 
     def first(s, c):
-        forward(2, s)
-        score_step(0, s - 1)
+        score_line(0, s - 1)
+        relay(3, s)
         return c
 
     lax.fori_loop(1, line, first, 0)
-    open_phase(3)
-    score_step(0, line - 1)
+    score_line(0, line - 1)
+    lax.fori_loop(0, line, lambda s, c: (score_across(0, s), c)[1], 0)
     reduce_open(0)
-
-    def second(s, c):
-        forward(3, s)
-        pl.when(s == 1)(lambda: reduce_core(0))
-        score_step(1, s - 1)
+    lax.fori_loop(0, line, lambda s, c: (score_line(1, s), c)[1], 0)
+    reduce_core(0)
+
+    def last(s, c):
+        score_across(1, s)
+        pl.when(s == line - 2)(lambda: reduce_close(0))
         return c
 
-    lax.fori_loop(1, line, second, 0)
-    reduce_close(0)
-    score_step(1, line - 1)
+    lax.fori_loop(0, line, last, 0)
     reduce_open(1)
     reduce_core(1)
     reduce_close(1)
 
     for phase in range(4):
+        each_on_line(lambda kk: along(phase, kk).wait_send())
 
         def drain(kk, c):
-            pl.when(has_right & (kk <= k))(
-                lambda: copy(phase, kk, RIGHT, right).wait_send()
-            )
-            pl.when(has_left & (kk >= k))(
-                lambda: copy(phase, kk, LEFT, left).wait_send()
-            )
-            copy(phase, kk, ACROSS, across).wait_send()
+            relay_copy(phase, kk).wait_send()
             return c
 
         lax.fori_loop(0, line, drain, 0)
@@ -285,7 +285,7 @@
             pltpu.VMEM((2, nq // 4, nt), bf16),
             pltpu.VMEM((2, nq // 4, nt), bf16),
             pltpu.SemaphoreType.DMA((4,)),
-            pltpu.SemaphoreType.DMA((4, 3, line)),
+            pltpu.SemaphoreType.DMA((4, 2, line)),
             pltpu.SemaphoreType.DMA((4, units)),
             pltpu.SemaphoreType.DMA((2, 2)),
             pltpu.SemaphoreType.DMA((2, 2)),

time: 73.2 us -> 80.1 us (1.094)
  Pallas kernels: 70.9 us -> 77.9 us
    pallas_call x1, Pallas kernels: 70.9 us -> 77.9 us  [per_device(): pl.pallas_call(functools.partial(kernel, line), out_shape=jax.ShapeDtypeS...]
where the time goes in v2:
time: 80.1 us; the launch traced here: 79.8 us
  Pallas kernels  77.9 us (97%)
  local copies, waits for them, and re-layouts  1.87 us (2%)
    pallas_call x1, Pallas kernels, per_device(): pl.pallas_call(functools.partial(kernel, line), out_shape=jax.ShapeDtypeS...  77.9 us
    unnamed x1, local copies, waits for them, and re-layouts  1.87 us

profile of v2, /device:TPU:0, one launch (start us, length us, event | category | flops | bytes accessed | tf_op | source)
XLA Modules:
  0.0 79.8 jit_solution(282992565142302457)
XLA Ops:
  0.0 77.9 %shard_map.37 = f32[2,2,16,2048]{3,2,1,0:T(8,128)} custom-call(bf16[2,16,4096]{2,1,0:T(8,128)(2,1)} %bitcast.7, bf16[4096,512]{1,0:T(8,128)(2,1)} %bitcast.5, bf16[2048,4096]{1,0:T(8,128)(2,1)} %bitcast.4), custom_call_target="tpu_custom_call" | custom-call | flops 5368709120 | bytes 20971520 | tf_op jit(solution)/shard_map/pallas_call | solution.py:272
  77.9 1.9 %copy.5 = f32[64,2048]{1,0:T(8,128)} copy(f32[64,2048]{1,0:T(8,128)} %bitcast.6) | data formatting | bytes 1048576

commit v3 on v1

--- a/solution.py
+++ b/solution.py
@@ -8,7 +8,7 @@
 from jax.sharding import PartitionSpec as P
 
 MESH = pl.DeviceIdType.MESH
-RIGHT, LEFT, ACROSS = 0, 1, 2
+RIGHT, LEFT, ACROSS, TWICE = 0, 1, 2, 3
 
 
 def kernel(
@@ -23,7 +23,6 @@
     width = cbuf.shape[3]
     nq = units * half_rows
     features, nt = tv.shape[1], tv.shape[0]
-    has_right, has_left = k + 1 < line, k > 0
 
     def at_row(r):
         return {"rows": r, "layers": layer}
@@ -32,6 +31,7 @@
         return {"rows": row, "layers": l}
 
     right, left, across = at_row(row + 2), at_row(row - 2), at_row(2 * k + 1 - y)
+    has_right, has_left = k + 1 < line, k > 0
     core_mate = at_layer(2 * x + 1 - core)
     x_mate = at_layer(2 * (1 - x) + core)
 
@@ -64,16 +64,18 @@
         return (qbuf if phase < 2 else cbuf).at[phase % 2, unit]
 
     def copy(phase, kk, side, target, own=False):
-        unit = 2 * kk + y
-        src = q_hbm.at[phase] if own and phase < 2 else slot(phase, unit)
+        unit = 2 * kk + (1 - y if side == TWICE else y)
         return pltpu.make_async_remote_copy(
-            src_ref=src,
+            src_ref=q_hbm.at[phase] if own and phase < 2 else slot(phase, unit),
             dst_ref=slot(phase, unit),
             send_sem=send_sem.at[phase, side, kk],
             recv_sem=recv_sem.at[phase, unit],
             device_id=target,
             device_id_type=MESH,
         )
+
+    def twice(phase):
+        return 0 if phase % 2 == 0 else line - 1
 
     def wait_unit(phase, unit):
         pltpu.make_async_remote_copy(
@@ -86,44 +88,37 @@
         ).wait_recv()
 
     def open_phase(phase):
-        @pl.when(has_right)
+        pl.when(has_right)(lambda: copy(phase, k, RIGHT, right, own=True).start())
+        pl.when(has_left)(lambda: copy(phase, k, LEFT, left, own=True).start())
+        copy(phase, k, ACROSS, across, own=True).start()
+
+    def forward(phase, s):
+        def onward(kk, side, target, more):
+            wait_unit(phase, 2 * kk + y)
+            pl.when(more)(lambda: copy(phase, kk, side, target).start())
+            pl.when(kk != twice(phase))(lambda: copy(phase, kk, ACROSS, across).start())
+
+        pl.when(k - s >= 0)(lambda: onward(k - s, RIGHT, right, has_right))
+        pl.when(k + s < line)(lambda: onward(k + s, LEFT, left, has_left))
+        kk = twice(phase)
+        distance, side, target, more = (
+            (k, RIGHT, right, has_right) if kk == 0 else (kk - k, LEFT, left, has_left)
+        )
+
+        @pl.when(s == distance + 1)
         def _():
-            copy(phase, k, RIGHT, right, own=True).start()
-
-        @pl.when(has_left)
-        def _():
-            copy(phase, k, LEFT, left, own=True).start()
-
-        copy(phase, k, ACROSS, across, own=True).start()
-
-    def forward(phase, s):
-        @pl.when(k - s >= 0)
-        def _():
-            wait_unit(phase, 2 * (k - s) + y)
-
-            @pl.when(has_right)
-            def _():
-                copy(phase, k - s, RIGHT, right).start()
-
-            copy(phase, k - s, ACROSS, across).start()
-
-        @pl.when(k + s < line)
-        def _():
-            wait_unit(phase, 2 * (k + s) + y)
-
-            @pl.when(has_left)
-            def _():
-                copy(phase, k + s, LEFT, left).start()
-
-            copy(phase, k + s, ACROSS, across).start()
-
-    def forward_all(phase):
-        lax.fori_loop(1, line, lambda s, c: (forward(phase, s), c)[1], 0)
+            wait_unit(phase, 2 * kk + 1 - y)
+            pl.when(more)(lambda: copy(phase, kk, TWICE, target).start())
 
     def wait_across(phase):
-        lax.fori_loop(
-            0, line, lambda kk, c: (wait_unit(phase, 2 * kk + 1 - y), c)[1], 0
-        )
+        def body(kk, c):
+            pl.when(kk != twice(phase))(lambda: wait_unit(phase, 2 * kk + 1 - y))
+            return c
+
+        lax.fori_loop(0, line, body, 0)
+
+    def forward_rest(phase, start):
+        lax.fori_loop(start, line + 1, lambda s, c: (forward(phase, s), c)[1], 0)
 
     depth = min(512, features)
 
@@ -157,14 +152,17 @@
 
         lax.fori_loop(0, nt // tile, body, 0)
 
-    def score_step(h, s):
-        def both(kk):
-            score(h, 2 * kk + y)
-            wait_unit(2 + h, 2 * kk + 1 - y)
+    def score_line(h, s):
+        pl.when(k - s >= 0)(lambda: score(h, 2 * (k - s) + y))
+        pl.when((s > 0) & (k + s < line))(lambda: score(h, 2 * (k + s) + y))
+
+    def score_across(h, s):
+        def one(kk):
+            pl.when(kk != twice(h))(lambda: wait_unit(2 + h, 2 * kk + 1 - y))
             score(h, 2 * kk + 1 - y)
 
-        pl.when(k - s >= 0)(lambda: both(k - s))
-        pl.when((s > 0) & (k + s < line))(lambda: both(k + s))
+        pl.when(k - s >= 0)(lambda: one(k - s))
+        pl.when((s > 0) & (k + s < line))(lambda: one(k + s))
 
     def core_copy(h, xx):
         return pltpu.make_async_remote_copy(
@@ -204,38 +202,44 @@
     open_phase(0)
     load_t.start()
     acc[...] = jnp.zeros_like(acc)
-    forward_all(0)
+    forward(0, 1)
+    forward(0, 2)
     open_phase(1)
+    forward_rest(0, 3)
     load_q[0].wait()
     load_p.wait()
+    forward(1, 1)
     wait_across(0)
+    forward(1, 2)
     condition(0)
-    forward_all(1)
     open_phase(2)
+    forward_rest(1, 3)
     load_q[1].wait()
     wait_across(1)
+    forward(2, 1)
     condition(1)
+    forward(2, 2)
+    open_phase(3)
+    forward_rest(2, 3)
     load_t.wait()
 
     def first(s, c):
-        forward(2, s)
-        score_step(0, s - 1)
+        score_line(0, s - 1)
+        forward(3, s)
         return c
 
-    lax.fori_loop(1, line, first, 0)
-    open_phase(3)
-    score_step(0, line - 1)
+    lax.fori_loop(1, line + 1, first, 0)
+    lax.fori_loop(0, line, lambda s, c: (score_across(0, s), c)[1], 0)
     reduce_open(0)
-
-    def second(s, c):
-        forward(3, s)
-        pl.when(s == 1)(lambda: reduce_core(0))
-        score_step(1, s - 1)
+    lax.fori_loop(0, line, lambda s, c: (score_line(1, s), c)[1], 0)
+    reduce_core(0)
+
+    def last(s, c):
+        score_across(1, s)
+        pl.when(s == line - 2)(lambda: reduce_close(0))
         return c
 
-    lax.fori_loop(1, line, second, 0)
-    reduce_close(0)
-    score_step(1, line - 1)
+    lax.fori_loop(0, line, last, 0)
     reduce_open(1)
     reduce_core(1)
     reduce_close(1)
@@ -249,10 +253,15 @@
             pl.when(has_left & (kk >= k))(
                 lambda: copy(phase, kk, LEFT, left).wait_send()
             )
-            copy(phase, kk, ACROSS, across).wait_send()
+            pl.when((kk == k) | (kk != twice(phase)))(
+                lambda: copy(phase, kk, ACROSS, across).wait_send()
+            )
             return c
 
         lax.fori_loop(0, line, drain, 0)
+        pl.when(has_right if phase % 2 == 0 else has_left)(
+            lambda: copy(phase, twice(phase), TWICE, across).wait_send()
+        )
     for h in range(2):
         core_copy(h, x).wait_send()
         core_copy(h, 1 - x).wait_send()
@@ -285,7 +294,7 @@
             pltpu.VMEM((2, nq // 4, nt), bf16),
             pltpu.VMEM((2, nq // 4, nt), bf16),
             pltpu.SemaphoreType.DMA((4,)),
-            pltpu.SemaphoreType.DMA((4, 3, line)),
+            pltpu.SemaphoreType.DMA((4, 4, line)),
             pltpu.SemaphoreType.DMA((4, units)),
             pltpu.SemaphoreType.DMA((2, 2)),
             pltpu.SemaphoreType.DMA((2, 2)),

time: 73.2 us -> 87.2 us (1.19)
  the two profiles are of different devices: /device:TPU:0 before, /device:TPU:5 now
where the time goes in v3:
time: 87.2 us; the launch traced here: 87 us
  Pallas kernels  85.1 us (98%)
  local copies, waits for them, and re-layouts  1.87 us (2%)
    pallas_call x1, Pallas kernels, per_device(): pl.pallas_call(functools.partial(kernel, line), out_shape=jax.ShapeDtypeS...  85.1 us
    unnamed x1, local copies, waits for them, and re-layouts  1.87 us

profile of v3, /device:TPU:5, one launch (start us, length us, event | category | flops | bytes accessed | tf_op | source)
XLA Modules:
  0.0 87.0 jit_solution(16290618884011115192)
XLA Ops:
  0.0 85.1 %shard_map.37 = f32[2,2,16,2048]{3,2,1,0:T(8,128)} custom-call(bf16[2,16,4096]{2,1,0:T(8,128)(2,1)} %bitcast.7, bf16[4096,512]{1,0:T(8,128)(2,1)} %bitcast.5, bf16[2048,4096]{1,0:T(8,128)(2,1)} %bitcast.4), custom_call_target="tpu_custom_call" | custom-call | flops 5368709120 | bytes 20971520 | tf_op jit(solution)/shard_map/pallas_call | solution.py:281
  85.1 1.9 %copy.5 = f32[64,2048]{1,0:T(8,128)} copy(f32[64,2048]{1,0:T(8,128)} %bitcast.6) | data formatting | bytes 1048576

commit v4 on v3

--- a/solution.py
+++ b/solution.py
@@ -8,7 +8,7 @@
 from jax.sharding import PartitionSpec as P
 
 MESH = pl.DeviceIdType.MESH
-RIGHT, LEFT, ACROSS, TWICE = 0, 1, 2, 3
+RIGHT, LEFT, ACROSS = 0, 1, 2
 
 
 def kernel(
@@ -64,7 +64,7 @@
         return (qbuf if phase < 2 else cbuf).at[phase % 2, unit]
 
     def copy(phase, kk, side, target, own=False):
-        unit = 2 * kk + (1 - y if side == TWICE else y)
+        unit = 2 * kk + y
         return pltpu.make_async_remote_copy(
             src_ref=q_hbm.at[phase] if own and phase < 2 else slot(phase, unit),
             dst_ref=slot(phase, unit),
@@ -73,9 +73,6 @@
             device_id=target,
             device_id_type=MESH,
         )
-
-    def twice(phase):
-        return 0 if phase % 2 == 0 else line - 1
 
     def wait_unit(phase, unit):
         pltpu.make_async_remote_copy(
@@ -96,29 +93,17 @@
         def onward(kk, side, target, more):
             wait_unit(phase, 2 * kk + y)
             pl.when(more)(lambda: copy(phase, kk, side, target).start())
-            pl.when(kk != twice(phase))(lambda: copy(phase, kk, ACROSS, across).start())
+            copy(phase, kk, ACROSS, across).start()
 
         pl.when(k - s >= 0)(lambda: onward(k - s, RIGHT, right, has_right))
         pl.when(k + s < line)(lambda: onward(k + s, LEFT, left, has_left))
-        kk = twice(phase)
-        distance, side, target, more = (
-            (k, RIGHT, right, has_right) if kk == 0 else (kk - k, LEFT, left, has_left)
-        )
-
-        @pl.when(s == distance + 1)
-        def _():
-            wait_unit(phase, 2 * kk + 1 - y)
-            pl.when(more)(lambda: copy(phase, kk, TWICE, target).start())
 
     def wait_across(phase):
         def body(kk, c):
-            pl.when(kk != twice(phase))(lambda: wait_unit(phase, 2 * kk + 1 - y))
+            wait_unit(phase, 2 * kk + 1 - y)
             return c
 
         lax.fori_loop(0, line, body, 0)
-
-    def forward_rest(phase, start):
-        lax.fori_loop(start, line + 1, lambda s, c: (forward(phase, s), c)[1], 0)
 
     depth = min(512, features)
 
@@ -158,7 +143,7 @@
 
     def score_across(h, s):
         def one(kk):
-            pl.when(kk != twice(h))(lambda: wait_unit(2 + h, 2 * kk + 1 - y))
+            wait_unit(2 + h, 2 * kk + 1 - y)
             score(h, 2 * kk + 1 - y)
 
         pl.when(k - s >= 0)(lambda: one(k - s))
@@ -200,49 +185,50 @@
         out_ref[:, h] = total.reshape(out_ref.shape[0], half_rows, nt)
 
     open_phase(0)
+    open_phase(1)
     load_t.start()
     acc[...] = jnp.zeros_like(acc)
-    forward(0, 1)
-    forward(0, 2)
-    open_phase(1)
-    forward_rest(0, 3)
+
+    def gather(s, c):
+        forward(0, s)
+        forward(1, s)
+        return c
+
+    lax.fori_loop(1, line, gather, 0)
     load_q[0].wait()
+    load_q[1].wait()
     load_p.wait()
-    forward(1, 1)
     wait_across(0)
-    forward(1, 2)
     condition(0)
     open_phase(2)
-    forward_rest(1, 3)
-    load_q[1].wait()
     wait_across(1)
-    forward(2, 1)
     condition(1)
-    forward(2, 2)
     open_phase(3)
-    forward_rest(2, 3)
     load_t.wait()
 
-    def first(s, c):
+    def gather_and_score(s, c):
+        forward(2, s)
+        forward(3, s)
         score_line(0, s - 1)
-        forward(3, s)
+        score_line(1, s - 1)
         return c
 
-    lax.fori_loop(1, line + 1, first, 0)
-    lax.fori_loop(0, line, lambda s, c: (score_across(0, s), c)[1], 0)
-    reduce_open(0)
-    lax.fori_loop(0, line, lambda s, c: (score_line(1, s), c)[1], 0)
-    reduce_core(0)
-
-    def last(s, c):
+    lax.fori_loop(1, line, gather_and_score, 0)
+    score_line(0, line - 1)
+    score_line(1, line - 1)
+
+    def finish(s, c):
+        score_across(0, s)
+        pl.when(s == line - 1)(lambda: reduce_open(0))
         score_across(1, s)
-        pl.when(s == line - 2)(lambda: reduce_close(0))
         return c
 
-    lax.fori_loop(0, line, last, 0)
+    lax.fori_loop(0, line, finish, 0)
     reduce_open(1)
-    reduce_core(1)
-    reduce_close(1)
+    for h in range(2):
+        reduce_core(h)
+    for h in range(2):
+        reduce_close(h)
 
     for phase in range(4):
 
@@ -253,15 +239,10 @@
             pl.when(has_left & (kk >= k))(
                 lambda: copy(phase, kk, LEFT, left).wait_send()
             )
-            pl.when((kk == k) | (kk != twice(phase)))(
-                lambda: copy(phase, kk, ACROSS, across).wait_send()
-            )
+            copy(phase, kk, ACROSS, across).wait_send()
             return c
 
         lax.fori_loop(0, line, drain, 0)
-        pl.when(has_right if phase % 2 == 0 else has_left)(
-            lambda: copy(phase, twice(phase), TWICE, across).wait_send()
-        )
     for h in range(2):
         core_copy(h, x).wait_send()
         core_copy(h, 1 - x).wait_send()
@@ -294,7 +275,7 @@
             pltpu.VMEM((2, nq // 4, nt), bf16),
             pltpu.VMEM((2, nq // 4, nt), bf16),
             pltpu.SemaphoreType.DMA((4,)),
-            pltpu.SemaphoreType.DMA((4, 4, line)),
+            pltpu.SemaphoreType.DMA((4, 3, line)),
             pltpu.SemaphoreType.DMA((4, units)),
             pltpu.SemaphoreType.DMA((2, 2)),
             pltpu.SemaphoreType.DMA((2, 2)),

time: 87.2 us -> 73.7 us (0.85)
  the two profiles are of different devices: /device:TPU:5 before, /device:TPU:0 now
where the time goes in v4:
time: 73.7 us; the launch traced here: 73.5 us
  Pallas kernels  71.6 us (97%)
  local copies, waits for them, and re-layouts  1.87 us (3%)
    pallas_call x1, Pallas kernels, per_device(): pl.pallas_call(functools.partial(kernel, line), out_shape=jax.ShapeDtypeS...  71.6 us
    unnamed x1, local copies, waits for them, and re-layouts  1.87 us

profile of v4, /device:TPU:0, one launch (start us, length us, event | category | flops | bytes accessed | tf_op | source)
XLA Modules:
  0.0 73.5 jit_solution(5505827449962507695)
XLA Ops:
  0.0 71.6 %shard_map.37 = f32[2,2,16,2048]{3,2,1,0:T(8,128)} custom-call(bf16[2,16,4096]{2,1,0:T(8,128)(2,1)} %bitcast.7, bf16[4096,512]{1,0:T(8,128)(2,1)} %bitcast.5, bf16[2048,4096]{1,0:T(8,128)(2,1)} %bitcast.4), custom_call_target="tpu_custom_call" | custom-call | flops 5368709120 | bytes 20971520 | tf_op jit(solution)/shard_map/pallas_call | solution.py:262
  71.7 1.9 %copy.5 = f32[64,2048]{1,0:T(8,128)} copy(f32[64,2048]{1,0:T(8,128)} %bitcast.6) | data formatting | bytes 1048576

commit v5 on v4

--- a/solution.py
+++ b/solution.py
@@ -13,7 +13,7 @@
 
 def kernel(
     line, q_hbm, p_hbm, t_hbm, out_ref,
-    qbuf, cbuf, pv, tv, cacc, acc, crecv, xsend, xrecv,
+    qbuf, cbuf, pv, tv, cacc, turned, acc, crecv, xsend, xrecv,
     local_sem, send_sem, recv_sem, csend_sem, crecv_sem, xsend_sem, xrecv_sem,
 ):
     row, layer = lax.axis_index("rows"), lax.axis_index("layers")
@@ -61,7 +61,7 @@
     pl.semaphore_wait(barrier, 3 + neighbours)
 
     def slot(phase, unit):
-        return (qbuf if phase < 2 else cbuf).at[phase % 2, unit]
+        return qbuf.at[phase, unit] if phase < 2 else cbuf.at[unit, phase - 2]
 
     def copy(phase, kk, side, target, own=False):
         unit = 2 * kk + y
@@ -119,35 +119,44 @@
             return c
 
         lax.fori_loop(0, features // depth, body, 0)
-        cbuf[h, row] = cacc[...].astype(jnp.bfloat16)
+        cbuf[row, h] = cacc[...].astype(jnp.bfloat16)
 
     tile = min(512, nt)
 
-    def score(h, unit):
+    def score(unit):
         cols = pl.ds(pl.multiple_of(unit * width, width), width)
 
         def body(i, c):
             rows = pl.ds(pl.multiple_of(i * tile, tile), tile)
-            part = lax.dot_general(
-                cbuf[h, unit], tv[rows, cols], (((1,), (1,)), ((), ())),
-                preferred_element_type=jnp.float32,
+            turned[rows, :] += lax.dot_general(
+                tv[rows, cols], cbuf[unit].reshape(2 * nq, width),
+                (((1,), (1,)), ((), ())), preferred_element_type=jnp.float32,
             )
-            acc[h, :, :, rows] += part.reshape(4, nq // 4, tile)
             return c
 
         lax.fori_loop(0, nt // tile, body, 0)
 
-    def score_line(h, s):
-        pl.when(k - s >= 0)(lambda: score(h, 2 * (k - s) + y))
-        pl.when((s > 0) & (k + s < line))(lambda: score(h, 2 * (k + s) + y))
-
-    def score_across(h, s):
+    def score_line(s):
+        pl.when(k - s >= 0)(lambda: score(2 * (k - s) + y))
+        pl.when((s > 0) & (k + s < line))(lambda: score(2 * (k + s) + y))
+
+    def score_across(s):
         def one(kk):
-            wait_unit(2 + h, 2 * kk + 1 - y)
-            score(h, 2 * kk + 1 - y)
+            wait_unit(2, 2 * kk + 1 - y)
+            wait_unit(3, 2 * kk + 1 - y)
+            score(2 * kk + 1 - y)
 
         pl.when(k - s >= 0)(lambda: one(k - s))
         pl.when((s > 0) & (k + s < line))(lambda: one(k + s))
+
+    def turn(h):
+        def body(i, c):
+            rows = pl.ds(pl.multiple_of(i * tile, tile), tile)
+            part = turned[rows, h * nq:(h + 1) * nq].T
+            acc[h, :, :, rows] = part.reshape(4, nq // 4, tile)
+            return c
+
+        lax.fori_loop(0, nt // tile, body, 0)
 
     def core_copy(h, xx):
         return pltpu.make_async_remote_copy(
@@ -187,7 +196,7 @@
     open_phase(0)
     open_phase(1)
     load_t.start()
-    acc[...] = jnp.zeros_like(acc)
+    turned[...] = jnp.zeros_like(turned)
 
     def gather(s, c):
         forward(0, s)
@@ -209,22 +218,16 @@
     def gather_and_score(s, c):
         forward(2, s)
         forward(3, s)
-        score_line(0, s - 1)
-        score_line(1, s - 1)
+        score_line(s - 1)
         return c
 
     lax.fori_loop(1, line, gather_and_score, 0)
-    score_line(0, line - 1)
-    score_line(1, line - 1)
-
-    def finish(s, c):
-        score_across(0, s)
-        pl.when(s == line - 1)(lambda: reduce_open(0))
-        score_across(1, s)
-        return c
-
-    lax.fori_loop(0, line, finish, 0)
-    reduce_open(1)
+    score_line(line - 1)
+
+    lax.fori_loop(0, line, lambda s, c: (score_across(s), c)[1], 0)
+    for h in range(2):
+        turn(h)
+        reduce_open(h)
     for h in range(2):
         reduce_core(h)
     for h in range(2):
@@ -266,10 +269,11 @@
         out_specs=pl.BlockSpec(memory_space=pltpu.VMEM),
         scratch_shapes=[
             pltpu.VMEM((2, units, half_rows, features), bf16),
-            pltpu.VMEM((2, units, nq, width), bf16),
+            pltpu.VMEM((units, 2, nq, width), bf16),
             pltpu.VMEM((features, width), bf16),
             pltpu.VMEM((nt, features), bf16),
             pltpu.VMEM((nq, width), f32),
+            pltpu.VMEM((nt, 2 * nq), f32),
             pltpu.VMEM((2, 4, nq // 4, nt), f32),
             pltpu.VMEM((2, 2, nq // 4, nt), f32),
             pltpu.VMEM((2, nq // 4, nt), bf16),

time: 73.7 us -> 67.8 us (0.920)
  Pallas kernels: 71.6 us -> 65.8 us
    pallas_call x1, Pallas kernels: 71.6 us -> 65.8 us  [per_device(): pl.pallas_call(functools.partial(kernel, line), out_shape=jax.ShapeDtypeS...]
where the time goes in v5:
time: 67.8 us; the launch traced here: 67.6 us
  Pallas kernels  65.8 us (97%)
  local copies, waits for them, and re-layouts  1.87 us (3%)
    pallas_call x1, Pallas kernels, per_device(): pl.pallas_call(functools.partial(kernel, line), out_shape=jax.ShapeDtypeS...  65.8 us
    unnamed x1, local copies, waits for them, and re-layouts  1.87 us

profile of v5, /device:TPU:0, one launch (start us, length us, event | category | flops | bytes accessed | tf_op | source)
XLA Modules:
  0.0 67.6 jit_solution(13788313720959685486)
XLA Ops:
  0.0 65.8 %shard_map.37 = f32[2,2,16,2048]{3,2,1,0:T(8,128)} custom-call(bf16[2,16,4096]{2,1,0:T(8,128)(2,1)} %bitcast.7, bf16[4096,512]{1,0:T(8,128)(2,1)} %bitcast.5, bf16[2048,4096]{1,0:T(8,128)(2,1)} %bitcast.4), custom_call_target="tpu_custom_call" | custom-call | flops 5368709120 | bytes 20971520 | tf_op jit(solution)/shard_map/pallas_call | solution.py:265
  65.8 1.9 %copy.5 = f32[64,2048]{1,0:T(8,128)} copy(f32[64,2048]{1,0:T(8,128)} %bitcast.6) | data formatting | bytes 1048576

commit v6 on v5

--- a/solution.py
+++ b/solution.py
@@ -8,7 +8,7 @@
 from jax.sharding import PartitionSpec as P
 
 MESH = pl.DeviceIdType.MESH
-RIGHT, LEFT, ACROSS = 0, 1, 2
+RIGHT, LEFT, ACROSS, TWICE = 0, 1, 2, 3
 
 
 def kernel(
@@ -64,7 +64,7 @@
         return qbuf.at[phase, unit] if phase < 2 else cbuf.at[unit, phase - 2]
 
     def copy(phase, kk, side, target, own=False):
-        unit = 2 * kk + y
+        unit = 2 * kk + (1 - y if side == TWICE else y)
         return pltpu.make_async_remote_copy(
             src_ref=q_hbm.at[phase] if own and phase < 2 else slot(phase, unit),
             dst_ref=slot(phase, unit),
@@ -73,6 +73,9 @@
             device_id=target,
             device_id_type=MESH,
         )
+
+    def twice(phase):
+        return 0 if phase % 2 == 0 else line - 1
 
     def wait_unit(phase, unit):
         pltpu.make_async_remote_copy(
@@ -93,14 +96,23 @@
         def onward(kk, side, target, more):
             wait_unit(phase, 2 * kk + y)
             pl.when(more)(lambda: copy(phase, kk, side, target).start())
-            copy(phase, kk, ACROSS, across).start()
+            pl.when(kk != twice(phase))(lambda: copy(phase, kk, ACROSS, across).start())
 
         pl.when(k - s >= 0)(lambda: onward(k - s, RIGHT, right, has_right))
         pl.when(k + s < line)(lambda: onward(k + s, LEFT, left, has_left))
+        end = twice(phase)
+        distance, side, target, more = (
+            (k, RIGHT, right, has_right) if end == 0 else (end - k, LEFT, left, has_left)
+        )
+
+        @pl.when(s == distance + 1)
+        def _():
+            wait_unit(phase, 2 * end + 1 - y)
+            pl.when(more)(lambda: copy(phase, end, TWICE, target).start())
 
     def wait_across(phase):
         def body(kk, c):
-            wait_unit(phase, 2 * kk + 1 - y)
+            pl.when(kk != twice(phase))(lambda: wait_unit(phase, 2 * kk + 1 - y))
             return c
 
         lax.fori_loop(0, line, body, 0)
@@ -142,8 +154,8 @@
 
     def score_across(s):
         def one(kk):
-            wait_unit(2, 2 * kk + 1 - y)
-            wait_unit(3, 2 * kk + 1 - y)
+            pl.when(kk != twice(2))(lambda: wait_unit(2, 2 * kk + 1 - y))
+            pl.when(kk != twice(3))(lambda: wait_unit(3, 2 * kk + 1 - y))
             score(2 * kk + 1 - y)
 
         pl.when(k - s >= 0)(lambda: one(k - s))
@@ -203,7 +215,7 @@
         forward(1, s)
         return c
 
-    lax.fori_loop(1, line, gather, 0)
+    lax.fori_loop(1, line + 1, gather, 0)
     load_q[0].wait()
     load_q[1].wait()
     load_p.wait()
@@ -221,8 +233,7 @@
         score_line(s - 1)
         return c
 
-    lax.fori_loop(1, line, gather_and_score, 0)
-    score_line(line - 1)
+    lax.fori_loop(1, line + 1, gather_and_score, 0)
 
     lax.fori_loop(0, line, lambda s, c: (score_across(s), c)[1], 0)
     for h in range(2):
@@ -242,10 +253,15 @@
             pl.when(has_left & (kk >= k))(
                 lambda: copy(phase, kk, LEFT, left).wait_send()
             )
-            copy(phase, kk, ACROSS, across).wait_send()
+            pl.when((kk == k) | (kk != twice(phase)))(
+                lambda: copy(phase, kk, ACROSS, across).wait_send()
+            )
             return c
 
         lax.fori_loop(0, line, drain, 0)
+        pl.when(has_right if phase % 2 == 0 else has_left)(
+            lambda: copy(phase, twice(phase), TWICE, across).wait_send()
+        )
     for h in range(2):
         core_copy(h, x).wait_send()
         core_copy(h, 1 - x).wait_send()
@@ -279,7 +295,7 @@
             pltpu.VMEM((2, nq // 4, nt), bf16),
             pltpu.VMEM((2, nq // 4, nt), bf16),
             pltpu.SemaphoreType.DMA((4,)),
-            pltpu.SemaphoreType.DMA((4, 3, line)),
+            pltpu.SemaphoreType.DMA((4, 4, line)),
             pltpu.SemaphoreType.DMA((4, units)),
             pltpu.SemaphoreType.DMA((2, 2)),
             pltpu.SemaphoreType.DMA((2, 2)),

time: 67.8 us -> 69.3 us (1.022)
  Pallas kernels: 65.8 us -> 67.3 us
    pallas_call x1, Pallas kernels: 65.8 us -> 67.3 us  [per_device(): pl.pallas_call(functools.partial(kernel, line), out_shape=jax.ShapeDtypeS...]
where the time goes in v6:
time: 69.3 us; the launch traced here: 69.2 us
  Pallas kernels  67.3 us (97%)
  local copies, waits for them, and re-layouts  1.87 us (3%)
    pallas_call x1, Pallas kernels, per_device(): pl.pallas_call(functools.partial(kernel, line), out_shape=jax.ShapeDtypeS...  67.3 us
    unnamed x1, local copies, waits for them, and re-layouts  1.87 us

profile of v6, /device:TPU:0, one launch (start us, length us, event | category | flops | bytes accessed | tf_op | source)
XLA Modules:
  0.0 69.2 jit_solution(6261460019601654807)
XLA Ops:
  0.0 67.3 %shard_map.37 = f32[2,2,16,2048]{3,2,1,0:T(8,128)} custom-call(bf16[2,16,4096]{2,1,0:T(8,128)(2,1)} %bitcast.7, bf16[4096,512]{1,0:T(8,128)(2,1)} %bitcast.5, bf16[2048,4096]{1,0:T(8,128)(2,1)} %bitcast.4), custom_call_target="tpu_custom_call" | custom-call | flops 5368709120 | bytes 20971520 | tf_op jit(solution)/shard_map/pallas_call | solution.py:281
  67.3 1.9 %copy.5 = f32[64,2048]{1,0:T(8,128)} copy(f32[64,2048]{1,0:T(8,128)} %bitcast.6) | data formatting | bytes 1048576

commit v7 on v5

--- a/solution.py
+++ b/solution.py
@@ -105,7 +105,7 @@
 
         lax.fori_loop(0, line, body, 0)
 
-    depth = min(512, features)
+    depth = min(2048, features)
 
     def condition(h):
         cacc[...] = jnp.zeros_like(cacc)

time: 67.8 us -> 66.8 us (0.985)
  Pallas kernels: 65.8 us -> 64.8 us
    pallas_call x1, Pallas kernels: 65.8 us -> 64.8 us  [per_device(): pl.pallas_call(functools.partial(kernel, line), out_shape=jax.ShapeDtypeS...]
where the time goes in v7:
time: 66.8 us; the launch traced here: 66.7 us
  Pallas kernels  64.8 us (97%)
  local copies, waits for them, and re-layouts  1.87 us (3%)
    pallas_call x1, Pallas kernels, per_device(): pl.pallas_call(functools.partial(kernel, line), out_shape=jax.ShapeDtypeS...  64.8 us
    unnamed x1, local copies, waits for them, and re-layouts  1.87 us

profile of v7, /device:TPU:0, one launch (start us, length us, event | category | flops | bytes accessed | tf_op | source)
XLA Modules:
  0.0 66.7 jit_solution(11286250513269949754)
XLA Ops:
  0.0 64.8 %shard_map.37 = f32[2,2,16,2048]{3,2,1,0:T(8,128)} custom-call(bf16[2,16,4096]{2,1,0:T(8,128)(2,1)} %bitcast.7, bf16[4096,512]{1,0:T(8,128)(2,1)} %bitcast.5, bf16[2048,4096]{1,0:T(8,128)(2,1)} %bitcast.4), custom_call_target="tpu_custom_call" | custom-call | flops 5368709120 | bytes 20971520 | tf_op jit(solution)/shard_map/pallas_call | solution.py:265
  64.8 1.9 %copy.5 = f32[64,2048]{1,0:T(8,128)} copy(f32[64,2048]{1,0:T(8,128)} %bitcast.6) | data formatting | bytes 1048576
